TPU v7x, 128 devices: a whole 4x4x4 slice. The times are simulated.
128 devices in a mesh: row: 16 (over x, z_hi, core), col: 8 (over z_lo, y).
Axes of the slice: x: 4, y: 4, z: 4 (z_hi: 2, z_lo: 2; z = z_hi * 2 + z_lo), core: 2. Of those that a mesh axis runs over, the one named last changes fastest.
Arguments:
- inputs: bfloat16 [2048, 8192], P('row', 'col'), may hold values from -6 to 6
- gate_pre: bfloat16 [2048, 26624], P('col', 'row'), may hold values from -6 to 6
- up_pre: bfloat16 [2048, 26624], P('col', 'row'), may hold values from -6 to 6
- grad_out: bfloat16 [2048, 8192], P('row', 'col'), may hold values from -0.3125 to 0.3125
- down_weight: bfloat16 [26624, 8192], P('row', 'col'), may hold values from -0.0625 to 0.0625
Outputs:
- grad_gate_weight: bfloat16 [8192, 26624], P('col', 'row')
- grad_up_weight: bfloat16 [8192, 26624], P('col', 'row')
- grad_down_weight: bfloat16 [26624, 8192], P('row', 'col')
All inputs are finite; a program needn't handle non-finite values.
Results may differ from a plain program's by a relative error of at most 0.0049.
Values may be sent and summed in bfloat16 or wider, within the bound.
A program may use at most 192 MiB of HBM per device.

v0:
```python
import jax
import jax.numpy as jnp
from jax import lax
from jax.sharding import PartitionSpec as P


def swiglu_backward(gate_pre, up_pre, grad_hidden):
    gate_value = gate_pre.astype(jnp.float32)
    up_value = up_pre.astype(jnp.float32)
    sigmoid_value = jax.nn.sigmoid(gate_value)
    silu_value = gate_value * sigmoid_value
    hidden = (silu_value * up_value).astype(jnp.bfloat16)
    grad_up = (grad_hidden * silu_value).astype(jnp.bfloat16)
    grad_gate = (
        grad_hidden * up_value * sigmoid_value * (1.0 + gate_value * (1.0 - sigmoid_value))
    ).astype(jnp.bfloat16)
    return (hidden, grad_gate, grad_up)


def contract_rows(left, right):
    return lax.dot_general(
        left, right, (((0,), (0,)), ((), ())), preferred_element_type=jnp.float32
    )


def contract_features(left, right):
    return lax.dot_general(
        left, right, (((1,), (1,)), ((), ())), preferred_element_type=jnp.float32
    )


def panel_grads(inputs_all, grad_all, gate_part, up_part, down_part):
    grad_hidden = lax.psum_scatter(
        contract_features(grad_all, down_part), "col", scatter_dimension=0, tiled=True
    )
    hidden, grad_gate, grad_up = swiglu_backward(gate_part, up_part, grad_hidden)
    return (
        contract_rows(lax.all_gather(hidden, "col", axis=0, tiled=True), grad_all),
        contract_rows(inputs_all, lax.all_gather(grad_gate, "col", axis=0, tiled=True)),
        contract_rows(inputs_all, lax.all_gather(grad_up, "col", axis=0, tiled=True)),
    )


def on_device(inputs, gate_pre, up_pre, grad_out, down_weight):
    inputs_all, grad_all = (
        lax.all_gather(inputs, "row", axis=0, tiled=True),
        lax.all_gather(grad_out, "row", axis=0, tiled=True),
    )
    down_list, gate_list, up_list = ([], [], [])
    down_part, gate_part, up_part = panel_grads(inputs_all, grad_all, gate_pre, up_pre, down_weight)
    down_list.append(down_part)
    gate_list.append(gate_part)
    up_list.append(up_part)
    down_total = down_list[0]
    gate_total = gate_list[0]
    up_total = up_list[0]
    return (
        gate_total.astype(jnp.bfloat16),
        up_total.astype(jnp.bfloat16),
        down_total.astype(jnp.bfloat16),
    )


def solution(mesh):
    placed = (P("row", "col"), P("col", "row"), P("col", "row"), P("row", "col"), P("row", "col"))
    return jax.shard_map(
        on_device,
        mesh=mesh,
        in_specs=placed,
        out_specs=(P("col", "row"), P("col", "row"), P("row", "col")),
        check_vma=False,
    )
```

profile of v0, /device:TPU:0, one launch (start us, length us, event | category | flops | bytes accessed | tf_op | source)
XLA Modules:
  0.0 532.4 jit_solution(6978633420390839282)
XLA Ops:
  7.2 0.0 all-gather.6.cloned.1.call-start
  7.2 0.7 all-gather.6.cloned.1.call-update
  7.9 0.0 reduce-scatter.2.cloned.1.call-start
  8.0 61.0 %all-gather.6.cloned.1.call-done = bf16[2048,1024]{1,0:T(8,128)(2,1)} async-done(((bf16[128,1024]{1,0:T(8,128)(2,1)}), bf16[2048,1024]{1,0:T(8,128)(2,1)}) %all-gather.6.cloned.1.call-update) | async-done | bytes 4194320 | tf_op jit(solution)/shard_map/all_gather | solution.py:47
  69.0 12.5 %fusion.10 = f32[2048,1664]{1,0:T(8,128)} fusion(bf16[2048,1024]{1,0:T(8,128)(2,1)} %all-gather.6.cloned.1.call-done, bf16[1664,1024]{1,0:T(8,128)(2,1)S(1)} %copy-done), kind=kOutput, calls=%fused_computation.19 | convolution fusion | flops 6979321856 | bytes 21233664 | tf_op jit(solution)/shard_map/dot_general | solution.py:27
  81.4 0.0 reduce-scatter.2.cloned.1.call-update
  81.5 0.0 all-gather.10.cloned.1.call-start
  81.5 0.7 all-gather.10.cloned.1.call-update
  82.2 0.0 all-gather.8.cloned.1.call-start
  82.2 140.2 %reduce-scatter.2.cloned.1.call-done = f32[256,1664]{1,0:T(8,128)} async-done(((f32[2048,1664]{1,0:T(8,128)}), f32[256,1664]{1,0:T(8,128)}) %reduce-scatter.2.cloned.1.call-update) | async-done | bytes 1703952 | tf_op jit(solution)/shard_map/reduce_scatter | solution.py:33
  222.5 3.8 multiply_convert_fusion
  226.3 0.0 all-gather.12.cloned.1.call-start
  226.4 0.5 all-gather.12.cloned.1.call-update
  226.9 0.2 all-gather.14.cloned.1.call-start
  227.1 0.3 all-gather.14.cloned.1.call-update
  227.5 52.2 %all-gather.10.cloned.1.call-done = bf16[2048,1024]{1,0:T(8,128)(2,1)} async-done(((bf16[128,1024]{1,0:T(8,128)(2,1)}), bf16[2048,1024]{1,0:T(8,128)(2,1)}) %all-gather.10.cloned.1.call-update) | async-done | bytes 4194320 | tf_op jit(solution)/shard_map/all_gather | solution.py:46
  279.7 78.0 %all-gather.8.cloned.1.call-done = bf16[2048,1664]{1,0:T(8,128)(2,1)} async-done(((bf16[256,1664]{1,0:T(8,128)(2,1)}), bf16[2048,1664]{1,0:T(8,128)(2,1)}) %all-gather.8.cloned.1.call-update) | async-done | bytes 6815760 | tf_op jit(solution)/shard_map/all_gather | solution.py:39
  357.7 11.1 %fusion = bf16[1024,1664]{0,1:T(8,128)(2,1)S(1)} fusion(bf16[2048,1664]{1,0:T(8,128)(2,1)} %all-gather.8.cloned.1.call-done, bf16[2048,1024]{1,0:T(8,128)(2,1)} %all-gather.10.cloned.1.call-done), kind=kOutput, calls=%fused_computation.3 | convolution fusion | flops 6981025792 | bytes 14417920 | tf_op jit(solution)/shard_map/dot_general | solution.py:21
  368.8 3.5 copy.8
  372.3 63.5 %all-gather.12.cloned.1.call-done = bf16[2048,1664]{1,0:T(8,128)(2,1)} async-done(((bf16[256,1664]{1,0:T(8,128)(2,1)}), bf16[2048,1664]{1,0:T(8,128)(2,1)}) %all-gather.12.cloned.1.call-update) | async-done | bytes 6815760 | tf_op jit(solution)/shard_map/all_gather | solution.py:40
  435.7 11.1 %fusion.1 = bf16[1024,1664]{0,1:T(8,128)(2,1)S(1)} fusion(bf16[2048,1664]{1,0:T(8,128)(2,1)} %all-gather.12.cloned.1.call-done, bf16[2048,1024]{1,0:T(8,128)(2,1)} %all-gather.10.cloned.1.call-done), kind=kOutput, calls=%fused_computation.4 | convolution fusion | flops 6981025792 | bytes 14417920 | tf_op jit(solution)/shard_map/dot_general | solution.py:21
  446.8 3.5 copy.9
  450.3 62.9 %all-gather.14.cloned.1.call-done = bf16[2048,1664]{1,0:T(8,128)(2,1)} async-done(((bf16[256,1664]{1,0:T(8,128)(2,1)}), bf16[2048,1664]{1,0:T(8,128)(2,1)}) %all-gather.14.cloned.1.call-update) | async-done | bytes 6815760 | tf_op jit(solution)/shard_map/all_gather | solution.py:38
  513.2 12.4 %convolution_convert_fusion = bf16[1664,1024]{1,0:T(8,128)(2,1)} fusion(bf16[2048,1664]{1,0:T(8,128)(2,1)} %all-gather.14.cloned.1.call-done, bf16[2048,1024]{1,0:T(8,128)(2,1)} %all-gather.6.cloned.1.call-done), kind=kOutput, calls=%fused_computation | convolution fusion | flops 6981025792 | bytes 14417920 | tf_op jit(solution)/shard_map/dot_general | solution.py:21
  (9 shorter events, 0.0 us)
Async XLA Ops:
  7.2 61.8 %copy-start = (bf16[1664,1024]{1,0:T(8,128)(2,1)S(1)}, bf16[1664,1024]{1,0:T(8,128)(2,1)}, u32[]{:S(2)}) copy-start(bf16[1664,1024]{1,0:T(8,128)(2,1)} %param.9) | copy-start | bytes 10223620
  7.2 61.8 %all-gather.6.cloned.1.call-start = ((), (), s32[]{:S(2)}) async-start(), calls=%async_computation.1 | async-start | bytes 4456448 | tf_op jit(solution)/shard_map/all_gather | solution.py:47
  7.9 214.6 %reduce-scatter.2.cloned.1.call-start = ((), (), s32[]{:S(2)}) async-start(), calls=%async_computation.2 | async-start | bytes 15335424 | tf_op jit(solution)/shard_map/reduce_scatter | solution.py:33
  81.4 141.1 %copy-start.2 = (bf16[256,1664]{1,0:T(8,128)(2,1)S(1)}, bf16[256,1664]{1,0:T(8,128)(2,1)}, u32[]{:S(2)}) copy-start(bf16[256,1664]{1,0:T(8,128)(2,1)} %param.6) | copy-start | bytes 2555908
  81.4 141.1 %copy-start.3 = (bf16[256,1664]{1,0:T(8,128)(2,1)S(1)}, bf16[256,1664]{1,0:T(8,128)(2,1)}, u32[]{:S(2)}) copy-start(bf16[256,1664]{1,0:T(8,128)(2,1)} %param.7) | copy-start | bytes 2555908
  81.5 198.3 %all-gather.10.cloned.1.call-start = ((), (), s32[]{:S(2)}) async-start(), calls=%async_computation.4 | async-start | bytes 4456448 | tf_op jit(solution)/shard_map/all_gather | solution.py:46
  82.2 275.5 %all-gather.8.cloned.1.call-start = ((), (), s32[]{:S(2)}) async-start(), calls=%async_computation.3 | async-start | bytes 7667712 | tf_op jit(solution)/shard_map/all_gather | solution.py:39
  226.3 209.4 %all-gather.12.cloned.1.call-start = ((), (), s32[]{:S(2)}) async-start(), calls=%async_computation.5 | async-start | bytes 7667712 | tf_op jit(solution)/shard_map/all_gather | solution.py:40
  226.9 286.3 %all-gather.14.cloned.1.call-start = ((), (), s32[]{:S(2)}) async-start(), calls=%async_computation.6 | async-start | bytes 7667712 | tf_op jit(solution)/shard_map/all_gather | solution.py:38
  513.2 12.4 %copy-start.1 = (bf16[1664,1024]{1,0:T(8,128)(2,1)S(1)}, bf16[1664,1024]{1,0:T(8,128)(2,1)}, u32[]{:S(2)}) copy-start(bf16[1664,1024]{1,0:T(8,128)(2,1)} %param.9) | copy-start | bytes 10223620
Sparse Core Ops, SparseCore 0:
  10.4 58.4 all-gather.5
  81.6 140.8 reduce-scatter.1
  224.9 54.7 all-gather.9
  281.8 75.8 all-gather.7
  359.7 75.9 all-gather.11
  437.2 75.9 all-gather.13
where the time goes:
time: 533 us; the launch traced here: 532 us
  waiting for transfers between devices  460 us (86%)
  matrix products  47 us (9%)
  between operations  14.1 us (3%)
  local copies, waits for them, and re-layouts  7.03 us (1%)
    reduce_scatter x1, waiting for transfers between devices, panel_grads(): lax.psum_scatter(contract_features(grad_all, down_part), 'col', scatter_d...  140 us
    all_gather x1, waiting for transfers between devices, panel_grads(): lax.all_gather(grad_gate, 'col', axis=0, tiled=True)  78 us
    all_gather x1, waiting for transfers between devices, panel_grads(): lax.all_gather(grad_up, 'col', axis=0, tiled=True)  63.5 us
    all_gather x1, waiting for transfers between devices, panel_grads(): lax.all_gather(hidden, 'col', axis=0, tiled=True)  62.9 us
    all_gather x1, waiting for transfers between devices, on_device(): lax.all_gather(grad_out, 'row', axis=0, tiled=True)  61 us
    all_gather x1, waiting for transfers between devices, on_device(): lax.all_gather(inputs, 'row', axis=0, tiled=True)  52.2 us
    dot_general x3, matrix products, contract_rows(): lax.dot_general(left, right, (((0,), (0,)), ((), ())), preferred_element_...  34.5 us
    dot_general x1, matrix products, contract_features(): lax.dot_general(left, right, (((1,), (1,)), ((), ())), preferred_element_...  12.5 us
  transfers between devices with their start and end apart: 6, of which 6 were waited for; matrix products, arithmetic and copies ran while one was open for 6% of the time, Pallas kernels for 0%

commit v1 on v0

v1 whole, which is shorter than its diff:
```python
import functools

import jax
import jax.numpy as jnp
from jax import lax
from jax.experimental import pallas as pl
from jax.experimental.pallas import tpu as pltpu
from jax.sharding import PartitionSpec as P

MESH = pl.DeviceIdType.MESH
BF = jnp.bfloat16
F32 = jnp.float32

FF = 1664
D = 1024
TOK = 2048
B_CHUNKS = (256, 256)
A_CHUNKS = (256, 256, 128)
BW = sum(B_CHUNKS)
NB = 2 * BW
NA = sum(A_CHUNKS)
CHUNKS = B_CHUNKS + A_CHUNKS
W = BW + NA
OFFS = tuple(sum(CHUNKS[:i]) for i in range(len(CHUNKS)))
NK = len(CHUNKS)
assert NB + NA == FF
N_REMOTE = 190
N_LOCAL = 64


def is_b(k):
    return k < len(B_CHUNKS)


def kernel(
    x_hbm, gate_hbm, up_hbm, go_hbm, down_hbm,
    og_hbm, ou_hbm, od_hbm,
    grad, in_t, gate, up, gh, part, far, near, swap_s, swap_r, dn_b, dn_a,
    hid_t, gg, gu, x_in, x_t, st_g, st_u, st_d,
    send_sem, recv_sem, local_sem,
):
    r = lax.axis_index("row")
    c = lax.axis_index("col")
    x, zh, core = r // 4, (r // 2) % 2, r % 2
    zl, y = c // 4, c % 4
    z = zh * 2 + zl

    def dev(x_, y_, z_, core_):
        return (x_ * 4 + (z_ // 2) * 2 + core_, (z_ % 2) * 4 + y_)

    zp, zm, z2 = (dev(x, y, (z + d) % 4, core) for d in (1, 3, 2))
    xp, xm, x2 = (dev((x + d) % 4, y, z, core) for d in (1, 3, 2))
    yp, ym = (dev(x, (y + d) % 4, z, core) for d in (1, 3))
    sib = dev(x, y, z, 1 - core)
    mate = dev(x, y, zh * 2 + 1 - zl, core)
    y_prev, y_next, y_far = (y + 3) % 4, (y + 1) % 4, (y + 2) % 4

    barrier = pltpu.get_barrier_semaphore()
    peers = (zp, zm, z2, xp, xm, x2, yp, ym, sib)
    for peer in peers:
        pl.semaphore_signal(barrier, inc=1, device_id=peer, device_id_type=MESH)

    counts = {"remote": 0, "local": 0}
    started = []
    sent = set()

    def send(src, dst, to):
        i = counts["remote"]
        counts["remote"] += 1
        copy = pltpu.make_async_remote_copy(
            src_ref=src, dst_ref=dst, send_sem=send_sem.at[i], recv_sem=recv_sem.at[i],
            device_id=to, device_id_type=MESH,
        )
        copy.start()
        started.append(copy)
        return copy

    def local(src, dst):
        i = counts["local"]
        counts["local"] += 1
        copy = pltpu.make_async_copy(src, dst, local_sem.at[i])
        copy.start()
        return copy

    def al(v, n):
        return pl.multiple_of(v, n)

    def token_block(x_, zh_):
        return al(((x_ % 2) * 8 + zh_ * 4 + (x_ // 2) * 2 + core) * 128, 128)

    own_tok = token_block(x, zh)

    def rows_of(buf, tok, lanes):
        return buf.at[:, :, pl.ds(tok, 128)] if lanes else buf.at[:, pl.ds(tok, 128)]

    def one_of(buf, tok, lanes):
        return buf.at[zl, :, pl.ds(tok, 128)] if lanes else buf.at[zl, pl.ds(tok, 128)]

    def cols(k):
        return pl.ds(OFFS[k], CHUNKS[k])

    def out_at(k, plane):
        if is_b(k):
            return pl.ds(al(plane * BW + OFFS[k], 128), CHUNKS[k])
        return pl.ds(OFFS[k] + BW, CHUNKS[k])

    in_copy = local(x_hbm, x_in)
    own_grad = local(go_hbm, one_of(grad, own_tok, False))
    streams = {"g": (gate_hbm, gate), "u": (up_hbm, up)}
    own_chunk = {}
    z_chunk = {}
    ya_c, yb_c = {}, {}

    def load_chunk(s, k):
        hbm, buf = streams[s]
        own_chunk[s, k] = local(hbm.at[:, out_at(k, zl)], buf.at[y * 2 + zl, :, cols(k)])

    def z_send_chunk(s, k):
        hbm, buf = streams[s]
        z_chunk[s, k] = send(hbm.at[:, out_at(k, 1 - zl)], buf.at[y * 2 + zl, :, cols(k)], mate)

    for k in range(NK):
        for s in "gu":
            load_chunk(s, k)
    dn_copies = [
        local(down_hbm.at[pl.ds(al(zl * BW, 128), BW)], dn_b.at[zl]),
        local(down_hbm.at[pl.ds(NB, NA)], dn_a),
    ]

    pl.semaphore_wait(barrier, len(peers))

    def gather_a(buf, k):
        sl = buf.at[pl.ds(y * 2, 2), :, cols(k)]
        return send(sl, sl, yp), send(sl, sl, ym)

    def gather_b(buf, k, first):
        first[0].wait_recv()
        lo = buf.at[y_prev * 2, :, cols(k)]
        one = send(lo, lo, yp)
        first[1].wait_recv()
        hi = buf.at[y_next * 2 + 1, :, cols(k)]
        return one, send(hi, hi, ym)

    def ya(s, k):
        own_chunk[s, k].wait()
        z_chunk[s, k].wait_recv()
        ya_c[s, k] = gather_a(streams[s][1], k)

    def yb(s, k):
        yb_c[s, k] = gather_b(streams[s][1], k, ya_c[s, k])

    def yc(s, k):
        for copy in yb_c[s, k]:
            copy.wait_recv()

    def row_z(src, buf, lanes):
        dst = one_of(buf, own_tok, lanes)
        return [send(src, dst, to) for to in (zp, zm, z2)]

    def row_core(buf, x_, lanes):
        return [
            send(rows_of(buf, token_block(x_, q), lanes), rows_of(buf, token_block(x_, q), lanes), sib)
            for q in range(2)
        ]

    def row_x(buf, lanes, z_copies):
        for copy in z_copies:
            copy.wait_recv()
        out = []
        for to in (xp, xm, x2):
            out.append([
                send(rows_of(buf, token_block(x, q), lanes), rows_of(buf, token_block(x, q), lanes), to)
                for q in range(2)
            ])
        return out, row_core(buf, x, lanes)

    def row_forward(buf, lanes, x_copies, core_copies, j):
        for copy in x_copies[j]:
            copy.wait_recv()
        core_copies += row_core(buf, (x + (3, 1, 2)[j]) % 4, lanes)

    def silu_parts(t, k):
        g = gate[t, :, cols(k)].astype(F32)
        u = up[t, :, cols(k)].astype(F32)
        s = jax.nn.sigmoid(g)
        return g, u, s

    def make_hidden(k):
        yc("g", k)
        yc("u", k)

        def body(t, carry):
            g, u, s = silu_parts(t, k)
            h = (g * s * u).astype(BF)
            hid_t[cols(k), pl.ds(al(t * 256, 256), 256)] = h.T
            return carry

        lax.fori_loop(0, 8, body, 0)

    def nt(a, b):
        return lax.dot_general(a, b, (((1,), (1,)), ((), ())), preferred_element_type=F32)

    def make_partial(k):
        n = CHUNKS[k]

        def body(t, carry):
            rows = pl.ds(al(t * 256, 256), 256)
            if is_b(k):
                acc = nt(grad[0, rows], dn_b[0, pl.ds(OFFS[k], n)])
                acc += nt(grad[1, rows], dn_b[1, pl.ds(OFFS[k], n)])
            else:
                acc = nt(grad[zl, rows], dn_a[pl.ds(OFFS[k] - BW, n)])
            part[t, :, cols(k)] = acc.astype(BF)
            return carry

        lax.fori_loop(0, 8, body, 0)

    rs1, rs2, swaps, ha, hb = {}, {}, {}, {}, {}

    def rs_a(k):
        make_partial(k)
        cc = cols(k)
        rs1[k] = (
            send(part.at[y_far * 2, :, cc], far.at[0, :, cc], yp),
            send(part.at[y_far * 2 + 1, :, cc], far.at[1, :, cc], ym),
            send(part.at[y_next * 2 + 1, :, cc], near.at[0, 1, :, cc], yp),
            send(part.at[y_prev * 2, :, cc], near.at[1, 0, :, cc], ym),
        )

    def rs_b(k):
        cc = cols(k)
        rs1[k][0].wait_recv()
        a = part[y_next * 2, :, cc].astype(F32) + far[0, :, cc].astype(F32)
        part[y_next * 2, :, cc] = a.astype(BF)
        one = send(part.at[y_next * 2, :, cc], near.at[0, 0, :, cc], yp)
        rs1[k][1].wait_recv()
        a = part[y_prev * 2 + 1, :, cc].astype(F32) + far[1, :, cc].astype(F32)
        part[y_prev * 2 + 1, :, cc] = a.astype(BF)
        rs2[k] = (one, send(part.at[y_prev * 2 + 1, :, cc], near.at[1, 1, :, cc], ym))

    def rs_c(k):
        cc = cols(k)
        for copy in (rs1[k][2], rs1[k][3], rs2[k][0], rs2[k][1]):
            copy.wait_recv()
        for q in range(2):
            a = part[y * 2 + q, :, cc].astype(F32)
            a += near[0, q, :, cc].astype(F32) + near[1, q, :, cc].astype(F32)
            if is_b(k):
                gh[y * 2 + q, :, cc] = a.astype(BF)
            else:
                swap_s[q, :, pl.ds(OFFS[k] - BW, CHUNKS[k])] = a.astype(BF)
        if is_b(k):
            ha[k] = gather_a(gh, k)
        else:
            sl = pl.ds(OFFS[k] - BW, CHUNKS[k])
            swaps[k] = send(swap_s.at[:, :, sl], swap_r.at[:, :, sl], mate)

    def rs_d(k):
        swaps[k].wait_recv()
        sl = pl.ds(OFFS[k] - BW, CHUNKS[k])
        for q in range(2):
            a = swap_s[q, :, sl].astype(F32) + swap_r[q, :, sl].astype(F32)
            gh[y * 2 + q, :, cols(k)] = a.astype(BF)
        ha[k] = gather_a(gh, k)

    def hg_b(k):
        hb[k] = gather_b(gh, k, ha[k])

    staged = {}

    def halves(k):
        return (zl, 1 - zl) if is_b(k) else (zl,)

    def clear(kind, k):
        for copy, is_remote in staged.pop((kind, k - 2), ()):
            if is_remote:
                copy.wait_send()
                sent.add(id(copy))
            else:
                copy.wait()

    def ship(kind, k, st, out, by_rows):
        n = CHUNKS[k]
        p = k % 2
        res = []
        for i in range(len(halves(k))):
            src = st.at[p, i, pl.ds(0, n), :] if by_rows else st.at[p, i, :, pl.ds(0, n)]
            dst = out.at[out_at(k, zl), :] if by_rows else out.at[:, out_at(k, zl)]
            res.append((local(src, dst), False) if i == 0 else (send(src, dst, mate), True))
        staged[kind, k] = res

    returned = []

    def down_grad(k):
        clear("d", k)
        n = CHUNKS[k]
        p = k % 2

        def body(m, carry):
            w = pl.ds(al(m * 256, 256), 256)
            for i, h in enumerate(halves(k)):
                acc = jnp.dot(hid_t[cols(k), :], grad[h, :, w], preferred_element_type=F32)
                st_d[p, i, pl.ds(0, n), w] = acc.astype(BF)
            return carry

        lax.fori_loop(0, 4, body, 0)
        ship("d", k, st_d, od_hbm, True)
        returned.extend(copy for copy, is_remote in staged["d", k] if is_remote)

    def weight_grads(k):
        for copy in hb[k]:
            copy.wait_recv()
        clear("g", k)
        clear("u", k)
        n = CHUNKS[k]
        p = k % 2

        def elem(t, carry):
            g, u, s = silu_parts(t, k)
            e = gh[t, :, cols(k)].astype(F32)
            rows = pl.ds(al(t * 256, 256), 256)
            gu[rows, pl.ds(0, n)] = (e * (g * s)).astype(BF)
            gg[rows, pl.ds(0, n)] = (e * u * s * (1.0 + g * (1.0 - s))).astype(BF)
            return carry

        lax.fori_loop(0, 8, elem, 0)

        def body(m, carry):
            w = pl.ds(al(m * 256, 256), 256)
            for i, h in enumerate(halves(k)):
                lhs = in_t[h, w, :]
                acc = jnp.dot(lhs, gg[:, pl.ds(0, n)], preferred_element_type=F32)
                st_g[p, i, w, pl.ds(0, n)] = acc.astype(BF)
                acc = jnp.dot(lhs, gu[:, pl.ds(0, n)], preferred_element_type=F32)
                st_u[p, i, w, pl.ds(0, n)] = acc.astype(BF)
            return carry

        lax.fori_loop(0, 4, body, 0)
        for kind, st, out in (("g", st_g, og_hbm), ("u", st_u, ou_hbm)):
            ship(kind, k, st, out, False)
            returned.extend(copy for copy, is_remote in staged[kind, k] if is_remote)

    z_send_chunk("g", 0)
    z_send_chunk("u", 0)
    grad_z = row_z(go_hbm, grad, False)
    z_send_chunk("g", 1)
    z_send_chunk("u", 1)
    in_copy.wait()
    x_t[...] = x_in[...].T
    own_in = local(x_t, one_of(in_t, own_tok, True))
    ya("g", 0)
    ya("u", 0)
    own_grad.wait()
    grad_x, grad_core = row_x(grad, False, grad_z)
    ya("g", 1)
    z_send_chunk("g", 2)
    z_send_chunk("u", 2)
    yb("g", 0)
    ya("u", 1)
    yb("u", 0)
    dn_z = send(down_hbm.at[pl.ds(al((1 - zl) * BW, 128), BW)], dn_b.at[zl], mate)
    ya("g", 2)
    yb("g", 1)
    z_send_chunk("g", 3)
    z_send_chunk("u", 3)
    make_hidden(0)
    ya("u", 2)
    yb("u", 1)
    z_send_chunk("g", 4)
    z_send_chunk("u", 4)
    in_z = row_z(x_t, in_t, True)
    ya("g", 3)
    yb("g", 2)
    row_forward(grad, False, grad_x, grad_core, 0)
    row_forward(grad, False, grad_x, grad_core, 1)
    ya("u", 3)
    yb("u", 2)
    make_hidden(1)
    row_forward(grad, False, grad_x, grad_core, 2)
    own_in.wait()
    in_x, in_core = row_x(in_t, True, in_z)
    for copy in dn_copies:
        copy.wait()
    dn_z.wait_recv()
    for copy in grad_core:
        copy.wait_recv()
    rs_a(0)
    ya("g", 4)
    yb("g", 3)
    rs_a(1)
    ya("u", 4)
    yb("u", 3)
    rs_b(0)
    rs_a(2)
    yb("g", 4)
    rs_b(1)
    yb("u", 4)
    rs_c(0)
    down_grad(0)
    rs_a(3)
    rs_b(2)
    rs_c(1)
    hg_b(0)
    down_grad(1)
    row_forward(in_t, True, in_x, in_core, 0)
    row_forward(in_t, True, in_x, in_core, 1)
    rs_a(4)
    rs_b(3)
    rs_c(2)
    hg_b(1)
    row_forward(in_t, True, in_x, in_core, 2)
    for copy in in_core:
        copy.wait_recv()
    weight_grads(0)
    rs_d(2)
    rs_b(4)
    rs_c(3)
    make_hidden(2)
    weight_grads(1)
    rs_d(3)
    hg_b(2)
    rs_c(4)
    make_hidden(3)
    down_grad(2)
    rs_d(4)
    hg_b(3)
    make_hidden(4)
    down_grad(3)
    weight_grads(2)
    hg_b(4)
    down_grad(4)
    weight_grads(3)
    weight_grads(4)

    for copies in staged.values():
        for copy, is_remote in copies:
            if not is_remote:
                copy.wait()
    for copy in returned:
        copy.wait_recv()
    for copy in started:
        if id(copy) not in sent:
            copy.wait_send()
    assert counts["remote"] <= N_REMOTE and counts["local"] <= N_LOCAL


def on_device(inputs, gate_pre, up_pre, grad_out, down_weight):
    any_spec = pl.BlockSpec(memory_space=pl.ANY)
    return pl.pallas_call(
        kernel,
        name="swiglu_backward",
        out_shape=(
            jax.ShapeDtypeStruct((D, FF), BF),
            jax.ShapeDtypeStruct((D, FF), BF),
            jax.ShapeDtypeStruct((FF, D), BF),
        ),
        in_specs=[any_spec] * 5,
        out_specs=(any_spec,) * 3,
        scratch_shapes=[
            pltpu.VMEM((2, TOK, D), BF),
            pltpu.VMEM((2, D, TOK), BF),
            pltpu.VMEM((8, 256, W), BF),
            pltpu.VMEM((8, 256, W), BF),
            pltpu.VMEM((8, 256, W), BF),
            pltpu.VMEM((8, 256, W), BF),
            pltpu.VMEM((2, 256, W), BF),
            pltpu.VMEM((2, 2, 256, W), BF),
            pltpu.VMEM((2, 256, NA), BF),
            pltpu.VMEM((2, 256, NA), BF),
            pltpu.VMEM((2, BW, D), BF),
            pltpu.VMEM((NA, D), BF),
            pltpu.VMEM((W, TOK), BF),
            pltpu.VMEM((TOK, 256), BF),
            pltpu.VMEM((TOK, 256), BF),
            pltpu.VMEM((128, D), BF),
            pltpu.VMEM((D, 128), BF),
            pltpu.VMEM((2, 2, D, 256), BF),
            pltpu.VMEM((2, 2, D, 256), BF),
            pltpu.VMEM((2, 2, 256, D), BF),
            pltpu.SemaphoreType.DMA((N_REMOTE,)),
            pltpu.SemaphoreType.DMA((N_REMOTE,)),
            pltpu.SemaphoreType.DMA((N_LOCAL,)),
        ],
        compiler_params=pltpu.CompilerParams(
            collective_id=0, has_side_effects=True, vmem_limit_bytes=62 * 2**20
        ),
        cost_estimate=pl.CostEstimate(
            flops=8 * TOK * D * FF, bytes_accessed=40 * 2**20, transcendentals=TOK * FF
        ),
    )(inputs, gate_pre, up_pre, grad_out, down_weight)


def solution(mesh):
    placed = (P("row", "col"), P("col", "row"), P("col", "row"), P("row", "col"), P("row", "col"))
    return jax.shard_map(
        on_device,
        mesh=mesh,
        in_specs=placed,
        out_specs=(P("col", "row"), P("col", "row"), P("row", "col")),
        check_vma=False,
    )
```

time: 533 us -> 237 us (0.44)
  waiting for transfers between devices: 460 us -> 0 us
  Pallas kernels: 0 us -> 227 us
  matrix products: 47 us -> 0 us
  between operations: 14.1 us -> 0.65 us
    all_gather x5 -> x0, waiting for transfers between devices: 318 us -> none  [the longest x1 78 us: panel_grads(): lax.all_gather(grad_gate, 'col', axis=0, tiled=True)]
    pallas_call x0 -> x1, Pallas kernels: none -> 227 us  [on_device(): pl.pallas_call(kernel, name='swiglu_backward', out_shape=(jax.ShapeDtypeS...]
    reduce_scatter x1 -> x0, waiting for transfers between devices: 140 us -> none  [panel_grads(): lax.psum_scatter(contract_features(grad_all, down_part), 'col', scatter_d...]
    dot_general x4 -> x0, matrix products: 47 us -> none  [the longest x3 34.5 us: contract_rows(): lax.dot_general(left, right, (((0,), (0,)), ((), ())), preferred_element_...]
  transfers between devices with their start and end apart: 6 -> 0, of which waited for: 6 -> 0; matrix products, arithmetic and copies ran while one was open for 6% -> 0% of each run, Pallas kernels for 0% -> 0%
where the time goes in v1:
time: 237 us
  Pallas kernels  227 us (96%)
  local copies, waits for them, and re-layouts  9.06 us (4%)
    pallas_call x1, Pallas kernels, on_device(): pl.pallas_call(kernel, name='swiglu_backward', out_shape=(jax.ShapeDtypeS...  227 us
    unnamed x7, local copies, waits for them, and re-layouts  9.06 us

profile of v1, /device:TPU:0, one launch (start us, length us, event | category | flops | bytes accessed | tf_op | source)
XLA Modules:
  0.0 236.7 jit_solution(6662685990397237248)
XLA Ops:
  0.6 227.0 %swiglu_backward.1 = (bf16[1024,1664]{1,0:T(8,128)(2,1)}, bf16[1024,1664]{1,0:T(8,128)(2,1)}, bf16[1664,1024]{1,0:T(8,128)(2,1)}) custom-call(bf16[128,1024]{1,0:T(8,128)(2,1)} %x_hbm.1, bf16[256,1664]{1,0:T(8,128)(2,1)} %gate_hbm.1, bf16[256,1664]{1,0:T(8,128)(2,1)} %up_hbm.1, bf16[128,1024]{1,0:T(8,128)(2,1)} %go_hbm.1, bf16[1664,1024]{1,0:T(8,128)(2,1)} %down_hbm.1), custom_call_target="tpu_custom_call" | custom-call | flops 27917287424 | bytes 41943040 | tf_op jit(solution)/shard_map/swiglu_backward/pallas_call | solution.py:449
  227.6 0.0 copy-start.1
  227.7 4.1 %copy.11 = bf16[1024,1664]{1,0:T(8,128)(2,1)} copy(bf16[1024,1664]{1,0:T(8,128)(2,1)} %get-tuple-element.6) | data formatting | bytes 6815744
  231.8 0.0 copy-done.1
  231.8 0.0 copy-start
  231.8 1.8 copy.12
  233.5 1.4 copy-done
  235.0 1.7 copy.13
Async XLA Ops:
  227.6 4.1 %copy-start.1 = (bf16[1024,1664]{1,0:T(8,128)(2,1)S(1)}, bf16[1024,1664]{1,0:T(8,128)(2,1)}, u32[]{:S(2)}) copy-start(bf16[1024,1664]{1,0:T(8,128)(2,1)} %get-tuple-element.7) | copy-start | bytes 10223620
  231.8 3.2 %copy-start = (bf16[1664,1024]{1,0:T(8,128)(2,1)S(1)}, bf16[1664,1024]{1,0:T(8,128)(2,1)}, u32[]{:S(2)}) copy-start(bf16[1664,1024]{1,0:T(8,128)(2,1)} %get-tuple-element.8) | copy-start | bytes 10223620

commit v2 on v1

--- a/solution.py
+++ b/solution.py
@@ -28,6 +28,19 @@
 N_LOCAL = 64
 
 
+SCHEDULE = (
+    "Zu1", "Au0", "Ag0", "Zg1", "gz0", "Au1", "Ag1", "Zg2", "Zu0", "Xg0",
+    "Bu1", "Zu2", "Bg1", "iz0", "Qu0", "Au2", "Fg0", "Ag2", "Zg0", "dz0",
+    "H1", "Bu2", "Xg1", "Lg0", "Qg0", "Eg0", "dw0", "P4", "P3", "Fg1",
+    "Bg0", "R4", "P2", "Lg1", "Xi0", "Bu0", "Eg1", "dw1", "D1", "P0",
+    "Zg3", "Zg4", "R3", "H0", "R0", "Zu4", "P1", "S4", "R2", "S0",
+    "S3", "Fi0", "S2", "Zu3", "R1", "G0", "Li0", "S1", "Bg2", "D0",
+    "T2", "Ag4", "Ei0", "O0", "G1", "G2", "H2", "Au3", "T4", "Ag3",
+    "Au4", "O1", "Bg4", "Bu4", "G4", "T3", "O2", "Bg3", "D2", "H4",
+    "Bu3", "D4", "O4", "G3", "H3", "D3", "O3",
+)
+
+
 def is_b(k):
     return k < len(B_CHUNKS)
 
@@ -35,7 +48,7 @@
 def kernel(
     x_hbm, gate_hbm, up_hbm, go_hbm, down_hbm,
     og_hbm, ou_hbm, od_hbm,
-    grad, in_t, gate, up, gh, part, far, near, swap_s, swap_r, dn_b, dn_a,
+    grad, in_t, gate, up, gh, part, kept, far, near, swap_s, swap_r, dn_b, dn_a,
     hid_t, gg, gu, x_in, x_t, st_g, st_u, st_d,
     send_sem, recv_sem, local_sem,
 ):
@@ -49,14 +62,14 @@
         return (x_ * 4 + (z_ // 2) * 2 + core_, (z_ % 2) * 4 + y_)
 
     zp, zm, z2 = (dev(x, y, (z + d) % 4, core) for d in (1, 3, 2))
-    xp, xm, x2 = (dev((x + d) % 4, y, z, core) for d in (1, 3, 2))
+    xp, xm = (dev((x + d) % 4, y, z, core) for d in (1, 3))
     yp, ym = (dev(x, (y + d) % 4, z, core) for d in (1, 3))
     sib = dev(x, y, z, 1 - core)
     mate = dev(x, y, zh * 2 + 1 - zl, core)
     y_prev, y_next, y_far = (y + 3) % 4, (y + 1) % 4, (y + 2) % 4
 
     barrier = pltpu.get_barrier_semaphore()
-    peers = (zp, zm, z2, xp, xm, x2, yp, ym, sib)
+    peers = (zp, zm, z2, xp, xm, yp, ym, sib)
     for peer in peers:
         pl.semaphore_signal(barrier, inc=1, device_id=peer, device_id_type=MESH)
 
@@ -142,12 +155,35 @@
         return one, send(hi, hi, ym)
 
     def ya(s, k):
+        hbm, buf = streams[s]
+        if k == 0:
+            dst = buf.at[y * 2 + zl, :, cols(k)]
+            src = hbm.at[:, out_at(k, zl)]
+            ya_c[s, k] = send(src, dst, yp), send(src, dst, ym)
+            return
         own_chunk[s, k].wait()
         z_chunk[s, k].wait_recv()
-        ya_c[s, k] = gather_a(streams[s][1], k)
+        ya_c[s, k] = gather_a(buf, k)
+
+    def yq(s, k):
+        buf = streams[s][1]
+        own_chunk[s, k].wait()
+        z_chunk[s, k].wait_recv()
+        other = buf.at[y * 2 + 1 - zl, :, cols(k)]
+        ya_c[s, k] += send(other, other, yp), send(other, other, ym)
 
     def yb(s, k):
-        yb_c[s, k] = gather_b(streams[s][1], k, ya_c[s, k])
+        buf = streams[s][1]
+        if k == 0:
+            own_p, own_m, other_p, other_m = ya_c[s, k]
+            own_p.wait_recv()
+            lo = buf.at[y_prev * 2 + zl, :, cols(k)]
+            one = send(lo, lo, yp)
+            other_m.wait_recv()
+            hi = buf.at[y_next * 2 + 1 - zl, :, cols(k)]
+            yb_c[s, k] = one, send(hi, hi, ym), own_m, other_p
+            return
+        yb_c[s, k] = gather_b(buf, k, ya_c[s, k])
 
     def yc(s, k):
         for copy in yb_c[s, k]:
@@ -155,29 +191,52 @@
 
     def row_z(src, buf, lanes):
         dst = one_of(buf, own_tok, lanes)
-        return [send(src, dst, to) for to in (zp, zm, z2)]
-
-    def row_core(buf, x_, lanes):
-        return [
-            send(rows_of(buf, token_block(x_, q), lanes), rows_of(buf, token_block(x_, q), lanes), sib)
-            for q in range(2)
-        ]
-
-    def row_x(buf, lanes, z_copies):
-        for copy in z_copies:
-            copy.wait_recv()
-        out = []
-        for to in (xp, xm, x2):
-            out.append([
-                send(rows_of(buf, token_block(x, q), lanes), rows_of(buf, token_block(x, q), lanes), to)
-                for q in range(2)
-            ])
-        return out, row_core(buf, x, lanes)
-
-    def row_forward(buf, lanes, x_copies, core_copies, j):
-        for copy in x_copies[j]:
-            copy.wait_recv()
-        core_copies += row_core(buf, (x + (3, 1, 2)[j]) % 4, lanes)
+        return [send(src, dst, to) for to in (z2, zp, zm)]
+
+    def block(buf, x_, q, which, lanes):
+        tok = pl.ds(token_block((x + x_) % 4, q), 128)
+        if which == "both":
+            return buf.at[:, :, tok] if lanes else buf.at[:, tok]
+        half = zl if which == "own" else 1 - zl
+        return buf.at[half, :, tok] if lanes else buf.at[half, tok]
+
+    class Row:
+        def __init__(self, buf, which, lanes):
+            self.buf, self.which, self.lanes = buf, which, lanes
+            self.core = []
+
+        def move(self, x_, q, to):
+            ref = block(self.buf, x_, q, self.which, self.lanes)
+            return send(ref, ref, to)
+
+        def to_core(self, x_):
+            self.core += [self.move(x_, q, sib) for q in range(2)]
+
+        def first(self, waits):
+            for wait in waits:
+                wait()
+            self.up = [self.move(0, q, xp) for q in range(2)]
+            self.down = [self.move(0, q, xm) for q in range(2)]
+            self.to_core(0)
+
+        def relay(self):
+            self.up[0].wait_recv()
+            self.far = [self.move(3, 0, xp)]
+            self.down[1].wait_recv()
+            self.far.append(self.move(1, 1, xm))
+            self.up[1].wait_recv()
+            self.to_core(3)
+            self.down[0].wait_recv()
+            self.to_core(1)
+
+        def last(self):
+            for copy in self.far:
+                copy.wait_recv()
+            self.to_core(2)
+
+        def done(self):
+            for copy in self.core:
+                copy.wait_recv()
 
     def silu_parts(t, k):
         g = gate[t, :, cols(k)].astype(F32)
@@ -200,25 +259,36 @@
     def nt(a, b):
         return lax.dot_general(a, b, (((1,), (1,)), ((), ())), preferred_element_type=F32)
 
-    def make_partial(k):
+    def partial_block(k, t):
         n = CHUNKS[k]
-
-        def body(t, carry):
-            rows = pl.ds(al(t * 256, 256), 256)
-            if is_b(k):
-                acc = nt(grad[0, rows], dn_b[0, pl.ds(OFFS[k], n)])
-                acc += nt(grad[1, rows], dn_b[1, pl.ds(OFFS[k], n)])
-            else:
-                acc = nt(grad[zl, rows], dn_a[pl.ds(OFFS[k] - BW, n)])
-            part[t, :, cols(k)] = acc.astype(BF)
+        rows = pl.ds(al(t * 256, 256), 256)
+        if is_b(k):
+            acc = nt(grad[0, rows], dn_b[0, pl.ds(OFFS[k], n)])
+            return acc + nt(grad[1, rows], dn_b[1, pl.ds(OFFS[k], n)])
+        return nt(grad[zl, rows], dn_a[pl.ds(OFFS[k] - BW, n)])
+
+    def make_sent(k):
+        def body(i, carry):
+            d = 2 - (i // 2) * (1 - 2 * (i % 2))
+            t = ((y + d) % 4) * 2 + (i // 2 + i) % 2
+            part[t, :, cols(k)] = partial_block(k, t).astype(BF)
             return carry
 
-        lax.fori_loop(0, 8, body, 0)
+        lax.fori_loop(0, 4, body, 0)
+
+    def make_kept(k):
+        def body(i, carry):
+            d = (i // 2) * (1 + 2 * (i % 2))
+            t = ((y + d) % 4) * 2 + i % 2
+            kept[i, :, cols(k)] = partial_block(k, t)
+            return carry
+
+        lax.fori_loop(0, 4, body, 0)
 
     rs1, rs2, swaps, ha, hb = {}, {}, {}, {}, {}
 
     def rs_a(k):
-        make_partial(k)
+        make_sent(k)
         cc = cols(k)
         rs1[k] = (
             send(part.at[y_far * 2, :, cc], far.at[0, :, cc], yp),
@@ -226,16 +296,15 @@
             send(part.at[y_next * 2 + 1, :, cc], near.at[0, 1, :, cc], yp),
             send(part.at[y_prev * 2, :, cc], near.at[1, 0, :, cc], ym),
         )
+        make_kept(k)
 
     def rs_b(k):
         cc = cols(k)
         rs1[k][0].wait_recv()
-        a = part[y_next * 2, :, cc].astype(F32) + far[0, :, cc].astype(F32)
-        part[y_next * 2, :, cc] = a.astype(BF)
+        part[y_next * 2, :, cc] = (kept[2, :, cc] + far[0, :, cc].astype(F32)).astype(BF)
         one = send(part.at[y_next * 2, :, cc], near.at[0, 0, :, cc], yp)
         rs1[k][1].wait_recv()
-        a = part[y_prev * 2 + 1, :, cc].astype(F32) + far[1, :, cc].astype(F32)
-        part[y_prev * 2 + 1, :, cc] = a.astype(BF)
+        part[y_prev * 2 + 1, :, cc] = (kept[3, :, cc] + far[1, :, cc].astype(F32)).astype(BF)
         rs2[k] = (one, send(part.at[y_prev * 2 + 1, :, cc], near.at[1, 1, :, cc], ym))
 
     def rs_c(k):
@@ -243,11 +312,11 @@
         for copy in (rs1[k][2], rs1[k][3], rs2[k][0], rs2[k][1]):
             copy.wait_recv()
         for q in range(2):
-            a = part[y * 2 + q, :, cc].astype(F32)
-            a += near[0, q, :, cc].astype(F32) + near[1, q, :, cc].astype(F32)
+            a = kept[q, :, cc] + near[0, q, :, cc].astype(F32) + near[1, q, :, cc].astype(F32)
             if is_b(k):
                 gh[y * 2 + q, :, cc] = a.astype(BF)
             else:
+                kept[q, :, cc] = a
                 swap_s[q, :, pl.ds(OFFS[k] - BW, CHUNKS[k])] = a.astype(BF)
         if is_b(k):
             ha[k] = gather_a(gh, k)
@@ -259,7 +328,7 @@
         swaps[k].wait_recv()
         sl = pl.ds(OFFS[k] - BW, CHUNKS[k])
         for q in range(2):
-            a = swap_s[q, :, sl].astype(F32) + swap_r[q, :, sl].astype(F32)
+            a = kept[q, :, cols(k)] + swap_r[q, :, sl].astype(F32)
             gh[y * 2 + q, :, cols(k)] = a.astype(BF)
         ha[k] = gather_a(gh, k)
 
@@ -340,97 +409,57 @@
             ship(kind, k, st, out, False)
             returned.extend(copy for copy, is_remote in staged[kind, k] if is_remote)
 
-    z_send_chunk("g", 0)
-    z_send_chunk("u", 0)
-    grad_z = row_z(go_hbm, grad, False)
-    z_send_chunk("g", 1)
-    z_send_chunk("u", 1)
-    in_copy.wait()
-    x_t[...] = x_in[...].T
-    own_in = local(x_t, one_of(in_t, own_tok, True))
-    ya("g", 0)
-    ya("u", 0)
-    own_grad.wait()
-    grad_x, grad_core = row_x(grad, False, grad_z)
-    ya("g", 1)
-    z_send_chunk("g", 2)
-    z_send_chunk("u", 2)
-    yb("g", 0)
-    ya("u", 1)
-    yb("u", 0)
-    dn_z = send(down_hbm.at[pl.ds(al((1 - zl) * BW, 128), BW)], dn_b.at[zl], mate)
-    ya("g", 2)
-    yb("g", 1)
-    z_send_chunk("g", 3)
-    z_send_chunk("u", 3)
-    make_hidden(0)
-    ya("u", 2)
-    yb("u", 1)
-    z_send_chunk("g", 4)
-    z_send_chunk("u", 4)
-    in_z = row_z(x_t, in_t, True)
-    ya("g", 3)
-    yb("g", 2)
-    row_forward(grad, False, grad_x, grad_core, 0)
-    row_forward(grad, False, grad_x, grad_core, 1)
-    ya("u", 3)
-    yb("u", 2)
-    make_hidden(1)
-    row_forward(grad, False, grad_x, grad_core, 2)
-    own_in.wait()
-    in_x, in_core = row_x(in_t, True, in_z)
-    for copy in dn_copies:
-        copy.wait()
-    dn_z.wait_recv()
-    for copy in grad_core:
-        copy.wait_recv()
-    rs_a(0)
-    ya("g", 4)
-    yb("g", 3)
-    rs_a(1)
-    ya("u", 4)
-    yb("u", 3)
-    rs_b(0)
-    rs_a(2)
-    yb("g", 4)
-    rs_b(1)
-    yb("u", 4)
-    rs_c(0)
-    down_grad(0)
-    rs_a(3)
-    rs_b(2)
-    rs_c(1)
-    hg_b(0)
-    down_grad(1)
-    row_forward(in_t, True, in_x, in_core, 0)
-    row_forward(in_t, True, in_x, in_core, 1)
-    rs_a(4)
-    rs_b(3)
-    rs_c(2)
-    hg_b(1)
-    row_forward(in_t, True, in_x, in_core, 2)
-    for copy in in_core:
-        copy.wait_recv()
-    weight_grads(0)
-    rs_d(2)
-    rs_b(4)
-    rs_c(3)
-    make_hidden(2)
-    weight_grads(1)
-    rs_d(3)
-    hg_b(2)
-    rs_c(4)
-    make_hidden(3)
-    down_grad(2)
-    rs_d(4)
-    hg_b(3)
-    make_hidden(4)
-    down_grad(3)
-    weight_grads(2)
-    hg_b(4)
-    down_grad(4)
-    weight_grads(3)
-    weight_grads(4)
+    rows = {
+        "g0": Row(grad, "own", False),
+        "g1": Row(grad, "other", False),
+        "i0": Row(in_t, "both", True),
+    }
+    zs = {}
+
+    def grad_z(k):
+        zs["g"] = row_z(go_hbm, grad, False)
+
+    def in_z(k):
+        in_copy.wait()
+        x_t[...] = x_in[...].T
+        zs["own"] = local(x_t, one_of(in_t, own_tok, True))
+        zs["i"] = row_z(x_t, in_t, True)
+
+    def row_first(s, k):
+        if s == "i":
+            waits = [zs["own"].wait] + [copy.wait_recv for copy in zs["i"]]
+        elif k == 0:
+            waits = [own_grad.wait, zs["g"][0].wait_recv]
+        else:
+            waits = [copy.wait_recv for copy in zs["g"][1:]]
+        rows[s + str(k)].first(waits)
+
+    def down_z(k):
+        zs["d"] = send(down_hbm.at[pl.ds(al((1 - zl) * BW, 128), BW)], dn_b.at[zl], mate)
+
+    def down_done(k):
+        if k == 0:
+            dn_copies[1].wait()
+        else:
+            dn_copies[0].wait()
+            zs["d"].wait_recv()
+
+    events = {
+        "Z": z_send_chunk, "A": ya, "Q": yq, "B": yb,
+        "X": row_first,
+        "F": lambda s, k: rows[s + str(k)].relay(),
+        "L": lambda s, k: rows[s + str(k)].last(),
+        "E": lambda s, k: rows[s + str(k)].done(),
+        "gz": grad_z, "iz": in_z, "dz": down_z, "dw": down_done,
+        "H": make_hidden, "P": rs_a, "R": rs_b, "S": rs_c, "T": rs_d, "G": hg_b,
+        "D": down_grad, "O": weight_grads,
+    }
+    for token in SCHEDULE:
+        name, k = token[:-1], int(token[-1])
+        if name in events:
+            events[name](k)
+        else:
+            events[name[0]](name[1], k)
 
     for copies in staged.values():
         for copy, is_remote in copies:
@@ -463,6 +492,7 @@
             pltpu.VMEM((8, 256, W), BF),
             pltpu.VMEM((8, 256, W), BF),
             pltpu.VMEM((8, 256, W), BF),
+            pltpu.VMEM((4, 256, W), F32),
             pltpu.VMEM((2, 256, W), BF),
             pltpu.VMEM((2, 2, 256, W), BF),
             pltpu.VMEM((2, 256, NA), BF),

time: 237 us -> 184 us (0.78)
  Pallas kernels: 227 us -> 174 us
    pallas_call x1, Pallas kernels: 227 us -> 174 us  [on_device(): pl.pallas_call(kernel, name='swiglu_backward', out_shape=(jax.ShapeDtypeS...]
where the time goes in v2:
time: 184 us
  Pallas kernels  174 us (95%)
  local copies, waits for them, and re-layouts  9.06 us (5%)
    pallas_call x1, Pallas kernels, on_device(): pl.pallas_call(kernel, name='swiglu_backward', out_shape=(jax.ShapeDtypeS...  174 us
    unnamed x7, local copies, waits for them, and re-layouts  9.06 us

profile of v2, /device:TPU:0, one launch (start us, length us, event | category | flops | bytes accessed | tf_op | source)
XLA Modules:
  0.0 184.1 jit_solution(2653673978997994938)
XLA Ops:
  0.6 174.4 %swiglu_backward.1 = (bf16[1024,1664]{1,0:T(8,128)(2,1)}, bf16[1024,1664]{1,0:T(8,128)(2,1)}, bf16[1664,1024]{1,0:T(8,128)(2,1)}) custom-call(bf16[128,1024]{1,0:T(8,128)(2,1)} %x_hbm.1, bf16[256,1664]{1,0:T(8,128)(2,1)} %gate_hbm.1, bf16[256,1664]{1,0:T(8,128)(2,1)} %up_hbm.1, bf16[128,1024]{1,0:T(8,128)(2,1)} %go_hbm.1, bf16[1664,1024]{1,0:T(8,128)(2,1)} %down_hbm.1), custom_call_target="tpu_custom_call" | custom-call | flops 27917287424 | bytes 41943040 | tf_op jit(solution)/shard_map/swiglu_backward/pallas_call | solution.py:478
  175.1 0.0 copy-start.1
  175.1 4.1 %copy.11 = bf16[1024,1664]{1,0:T(8,128)(2,1)} copy(bf16[1024,1664]{1,0:T(8,128)(2,1)} %get-tuple-element.6) | data formatting | bytes 6815744
  179.2 0.0 copy-done.1
  179.2 0.0 copy-start
  179.2 1.8 copy.12
  180.9 1.4 copy-done
  182.4 1.7 copy.13
Async XLA Ops:
  175.1 4.1 %copy-start.1 = (bf16[1024,1664]{1,0:T(8,128)(2,1)S(1)}, bf16[1024,1664]{1,0:T(8,128)(2,1)}, u32[]{:S(2)}) copy-start(bf16[1024,1664]{1,0:T(8,128)(2,1)} %get-tuple-element.7) | copy-start | bytes 10223620
  179.2 3.2 %copy-start = (bf16[1664,1024]{1,0:T(8,128)(2,1)S(1)}, bf16[1664,1024]{1,0:T(8,128)(2,1)}, u32[]{:S(2)}) copy-start(bf16[1664,1024]{1,0:T(8,128)(2,1)} %get-tuple-element.8) | copy-start | bytes 10223620

commit v3 on v2

--- a/solution.py
+++ b/solution.py
@@ -15,34 +15,44 @@
 D = 1024
 TOK = 2048
 B_CHUNKS = (256, 256)
-A_CHUNKS = (256, 256, 128)
+S_CHUNKS = (256,)
+A_CHUNKS = (256, 128)
 BW = sum(B_CHUNKS)
 NB = 2 * BW
-NA = sum(A_CHUNKS)
-CHUNKS = B_CHUNKS + A_CHUNKS
+NS = sum(S_CHUNKS)
+NA = NS + sum(A_CHUNKS)
+CHUNKS = B_CHUNKS + S_CHUNKS + A_CHUNKS
 W = BW + NA
 OFFS = tuple(sum(CHUNKS[:i]) for i in range(len(CHUNKS)))
 NK = len(CHUNKS)
 assert NB + NA == FF
-N_REMOTE = 190
-N_LOCAL = 64
+N_REMOTE = 166
+N_LOCAL = 40
 
 
 SCHEDULE = (
-    "Zu1", "Au0", "Ag0", "Zg1", "gz0", "Au1", "Ag1", "Zg2", "Zu0", "Xg0",
-    "Bu1", "Zu2", "Bg1", "iz0", "Qu0", "Au2", "Fg0", "Ag2", "Zg0", "dz0",
-    "H1", "Bu2", "Xg1", "Lg0", "Qg0", "Eg0", "dw0", "P4", "P3", "Fg1",
-    "Bg0", "R4", "P2", "Lg1", "Xi0", "Bu0", "Eg1", "dw1", "D1", "P0",
-    "Zg3", "Zg4", "R3", "H0", "R0", "Zu4", "P1", "S4", "R2", "S0",
-    "S3", "Fi0", "S2", "Zu3", "R1", "G0", "Li0", "S1", "Bg2", "D0",
-    "T2", "Ag4", "Ei0", "O0", "G1", "G2", "H2", "Au3", "T4", "Ag3",
-    "Au4", "O1", "Bg4", "Bu4", "G4", "T3", "O2", "Bg3", "D2", "H4",
-    "Bu3", "D4", "O4", "G3", "H3", "D3", "O3",
+    "Zu4", "Au0", "Zu1", "Ag0", "gz0", "Au4", "Au1", "Zg1", "gr0", "Zg0",
+    "Xg1", "Bu4", "Zu0", "Ag1", "Zg3", "Qg0", "iz0", "Zg2", "dz0", "Bu1",
+    "Ag3", "Qu0", "Bg1", "Xg0", "Fg0", "Bg0", "Bu0", "ir0", "Fg1", "Ag2",
+    "Lg0", "Eg0", "dw0", "P3", "H0", "H1", "Lg1", "Xi0", "P4", "R3",
+    "Zu2", "R4", "Eg1", "dw1", "P0", "S3", "P1", "Zg4", "Zu3", "D1",
+    "R0", "R1", "Fi0", "S0", "D0", "P2", "S4", "G0", "R2", "Li0",
+    "S1", "S2", "Au2", "Au3", "Ei0", "O0", "Bg3", "G1", "Bu3", "Bu2",
+    "Bg2", "T2", "O1", "Ag4", "H2", "D2", "G2", "H3", "T4", "Bg4",
+    "D3", "T3", "O2", "G4", "H4", "G3", "D4", "O4", "O3",
 )
 
 
 def is_b(k):
     return k < len(B_CHUNKS)
+
+
+def is_s(k):
+    return len(B_CHUNKS) <= k < len(B_CHUNKS) + len(S_CHUNKS)
+
+
+def rs_width(k):
+    return CHUNKS[k] // 2 if is_s(k) else CHUNKS[k]
 
 
 def kernel(
@@ -61,7 +71,7 @@
     def dev(x_, y_, z_, core_):
         return (x_ * 4 + (z_ // 2) * 2 + core_, (z_ % 2) * 4 + y_)
 
-    zp, zm, z2 = (dev(x, y, (z + d) % 4, core) for d in (1, 3, 2))
+    zo = dev(x, y, (1 - zh) * 2 + 1 - zl, core)
     xp, xm = (dev((x + d) % 4, y, z, core) for d in (1, 3))
     yp, ym = (dev(x, (y + d) % 4, z, core) for d in (1, 3))
     sib = dev(x, y, z, 1 - core)
@@ -69,7 +79,7 @@
     y_prev, y_next, y_far = (y + 3) % 4, (y + 1) % 4, (y + 2) % 4
 
     barrier = pltpu.get_barrier_semaphore()
-    peers = (zp, zm, z2, xp, xm, yp, ym, sib)
+    peers = (mate, zo, xp, xm, yp, ym, sib)
     for peer in peers:
         pl.semaphore_signal(barrier, inc=1, device_id=peer, device_id_type=MESH)
 
@@ -112,10 +122,30 @@
     def cols(k):
         return pl.ds(OFFS[k], CHUNKS[k])
 
+    def rcols(k):
+        return pl.ds(OFFS[k], rs_width(k))
+
+    def dn_at(k):
+        return OFFS[k] if is_b(k) else BW + (OFFS[k] - BW) // 2
+
+    def swap_cols(k):
+        return pl.ds(OFFS[k] - BW - NS, CHUNKS[k])
+
     def out_at(k, plane):
         if is_b(k):
             return pl.ds(al(plane * BW + OFFS[k], 128), CHUNKS[k])
         return pl.ds(OFFS[k] + BW, CHUNKS[k])
+
+    def down_parts(plane):
+        parts = [(pl.ds(al(plane * BW, 128), BW), pl.ds(0, BW))]
+        for k in range(NK):
+            if is_s(k):
+                n = CHUNKS[k] // 2
+                parts.append((
+                    pl.ds(al(BW + OFFS[k] + plane * n, 128), n),
+                    pl.ds(dn_at(k), n),
+                ))
+        return parts
 
     in_copy = local(x_hbm, x_in)
     own_grad = local(go_hbm, one_of(grad, own_tok, False))
@@ -136,9 +166,9 @@
         for s in "gu":
             load_chunk(s, k)
     dn_copies = [
-        local(down_hbm.at[pl.ds(al(zl * BW, 128), BW)], dn_b.at[zl]),
-        local(down_hbm.at[pl.ds(NB, NA)], dn_a),
+        local(down_hbm.at[src], dn_b.at[zl, dst]) for src, dst in down_parts(zl)
     ]
+    dn_copy_a = local(down_hbm.at[pl.ds(NB + NS, NA - NS)], dn_a)
 
     pl.semaphore_wait(barrier, len(peers))
 
@@ -191,7 +221,13 @@
 
     def row_z(src, buf, lanes):
         dst = one_of(buf, own_tok, lanes)
-        return [send(src, dst, to) for to in (z2, zp, zm)]
+        return [send(src, dst, to) for to in (mate, zo)]
+
+    def row_z_relay(buf, lanes, copies):
+        copies[0].wait_recv()
+        tok = pl.ds(own_tok, 128)
+        ref = buf.at[1 - zl, :, tok] if lanes else buf.at[1 - zl, tok]
+        copies.append(send(ref, ref, zo))
 
     def block(buf, x_, q, which, lanes):
         tok = pl.ds(token_block((x + x_) % 4, q), 128)
@@ -260,18 +296,18 @@
         return lax.dot_general(a, b, (((1,), (1,)), ((), ())), preferred_element_type=F32)
 
     def partial_block(k, t):
-        n = CHUNKS[k]
+        n = rs_width(k)
         rows = pl.ds(al(t * 256, 256), 256)
-        if is_b(k):
-            acc = nt(grad[0, rows], dn_b[0, pl.ds(OFFS[k], n)])
-            return acc + nt(grad[1, rows], dn_b[1, pl.ds(OFFS[k], n)])
-        return nt(grad[zl, rows], dn_a[pl.ds(OFFS[k] - BW, n)])
+        if is_b(k) or is_s(k):
+            acc = nt(grad[0, rows], dn_b[0, pl.ds(dn_at(k), n)])
+            return acc + nt(grad[1, rows], dn_b[1, pl.ds(dn_at(k), n)])
+        return nt(grad[zl, rows], dn_a[pl.ds(OFFS[k] - BW - NS, n)])
 
     def make_sent(k):
         def body(i, carry):
             d = 2 - (i // 2) * (1 - 2 * (i % 2))
             t = ((y + d) % 4) * 2 + (i // 2 + i) % 2
-            part[t, :, cols(k)] = partial_block(k, t).astype(BF)
+            part[t, :, rcols(k)] = partial_block(k, t).astype(BF)
             return carry
 
         lax.fori_loop(0, 4, body, 0)
@@ -280,7 +316,7 @@
         def body(i, carry):
             d = (i // 2) * (1 + 2 * (i % 2))
             t = ((y + d) % 4) * 2 + i % 2
-            kept[i, :, cols(k)] = partial_block(k, t)
+            kept[i, :, rcols(k)] = partial_block(k, t)
             return carry
 
         lax.fori_loop(0, 4, body, 0)
@@ -289,7 +325,7 @@
 
     def rs_a(k):
         make_sent(k)
-        cc = cols(k)
+        cc = rcols(k)
         rs1[k] = (
             send(part.at[y_far * 2, :, cc], far.at[0, :, cc], yp),
             send(part.at[y_far * 2 + 1, :, cc], far.at[1, :, cc], ym),
@@ -299,7 +335,7 @@
         make_kept(k)
 
     def rs_b(k):
-        cc = cols(k)
+        cc = rcols(k)
         rs1[k][0].wait_recv()
         part[y_next * 2, :, cc] = (kept[2, :, cc] + far[0, :, cc].astype(F32)).astype(BF)
         one = send(part.at[y_next * 2, :, cc], near.at[0, 0, :, cc], yp)
@@ -308,28 +344,35 @@
         rs2[k] = (one, send(part.at[y_prev * 2 + 1, :, cc], near.at[1, 1, :, cc], ym))
 
     def rs_c(k):
-        cc = cols(k)
+        cc = rcols(k)
+        n = rs_width(k)
         for copy in (rs1[k][2], rs1[k][3], rs2[k][0], rs2[k][1]):
             copy.wait_recv()
+        if is_s(k):
+            to = pl.ds(al(OFFS[k] + zl * n, 128), n)
+        elif is_b(k):
+            to = cols(k)
         for q in range(2):
             a = kept[q, :, cc] + near[0, q, :, cc].astype(F32) + near[1, q, :, cc].astype(F32)
-            if is_b(k):
-                gh[y * 2 + q, :, cc] = a.astype(BF)
+            if is_b(k) or is_s(k):
+                gh[y * 2 + q, :, to] = a.astype(BF)
             else:
                 kept[q, :, cc] = a
-                swap_s[q, :, pl.ds(OFFS[k] - BW, CHUNKS[k])] = a.astype(BF)
+                swap_s[q, :, swap_cols(k)] = a.astype(BF)
         if is_b(k):
             ha[k] = gather_a(gh, k)
+        elif is_s(k):
+            ref = gh.at[pl.ds(y * 2, 2), :, to]
+            swaps[k] = send(ref, ref, mate)
         else:
-            sl = pl.ds(OFFS[k] - BW, CHUNKS[k])
-            swaps[k] = send(swap_s.at[:, :, sl], swap_r.at[:, :, sl], mate)
+            swaps[k] = send(swap_s.at[:, :, swap_cols(k)], swap_r.at[:, :, swap_cols(k)], mate)
 
     def rs_d(k):
         swaps[k].wait_recv()
-        sl = pl.ds(OFFS[k] - BW, CHUNKS[k])
-        for q in range(2):
-            a = kept[q, :, cols(k)] + swap_r[q, :, sl].astype(F32)
-            gh[y * 2 + q, :, cols(k)] = a.astype(BF)
+        if not is_s(k):
+            for q in range(2):
+                a = kept[q, :, cols(k)] + swap_r[q, :, swap_cols(k)].astype(F32)
+                gh[y * 2 + q, :, cols(k)] = a.astype(BF)
         ha[k] = gather_a(gh, k)
 
     def hg_b(k):
@@ -366,13 +409,13 @@
         p = k % 2
 
         def body(m, carry):
-            w = pl.ds(al(m * 256, 256), 256)
+            w = pl.ds(al(m * 512, 512), 512)
             for i, h in enumerate(halves(k)):
                 acc = jnp.dot(hid_t[cols(k), :], grad[h, :, w], preferred_element_type=F32)
                 st_d[p, i, pl.ds(0, n), w] = acc.astype(BF)
             return carry
 
-        lax.fori_loop(0, 4, body, 0)
+        lax.fori_loop(0, 2, body, 0)
         ship("d", k, st_d, od_hbm, True)
         returned.extend(copy for copy, is_remote in staged["d", k] if is_remote)
 
@@ -395,7 +438,7 @@
         lax.fori_loop(0, 8, elem, 0)
 
         def body(m, carry):
-            w = pl.ds(al(m * 256, 256), 256)
+            w = pl.ds(al(m * 1024, 1024), 1024)
             for i, h in enumerate(halves(k)):
                 lhs = in_t[h, w, :]
                 acc = jnp.dot(lhs, gg[:, pl.ds(0, n)], preferred_element_type=F32)
@@ -404,7 +447,7 @@
                 st_u[p, i, w, pl.ds(0, n)] = acc.astype(BF)
             return carry
 
-        lax.fori_loop(0, 4, body, 0)
+        lax.fori_loop(0, 1, body, 0)
         for kind, st, out in (("g", st_g, og_hbm), ("u", st_u, ou_hbm)):
             ship(kind, k, st, out, False)
             returned.extend(copy for copy, is_remote in staged[kind, k] if is_remote)
@@ -427,22 +470,24 @@
 
     def row_first(s, k):
         if s == "i":
-            waits = [zs["own"].wait] + [copy.wait_recv for copy in zs["i"]]
+            waits = [zs["own"].wait] + [copy.wait_recv for copy in zs["i"][1:]]
         elif k == 0:
-            waits = [own_grad.wait, zs["g"][0].wait_recv]
+            waits = [own_grad.wait, zs["g"][2].wait_recv]
         else:
-            waits = [copy.wait_recv for copy in zs["g"][1:]]
+            waits = [zs["g"][1].wait_recv]
         rows[s + str(k)].first(waits)
 
     def down_z(k):
-        zs["d"] = send(down_hbm.at[pl.ds(al((1 - zl) * BW, 128), BW)], dn_b.at[zl], mate)
+        zs["d"] = [send(down_hbm.at[src], dn_b.at[zl, dst], mate) for src, dst in down_parts(1 - zl)]
 
     def down_done(k):
         if k == 0:
-            dn_copies[1].wait()
+            dn_copy_a.wait()
         else:
-            dn_copies[0].wait()
-            zs["d"].wait_recv()
+            for copy in dn_copies:
+                copy.wait()
+            for copy in zs["d"]:
+                copy.wait_recv()
 
     events = {
         "Z": z_send_chunk, "A": ya, "Q": yq, "B": yb,
@@ -450,6 +495,8 @@
         "F": lambda s, k: rows[s + str(k)].relay(),
         "L": lambda s, k: rows[s + str(k)].last(),
         "E": lambda s, k: rows[s + str(k)].done(),
+        "gr": lambda k: row_z_relay(grad, False, zs["g"]),
+        "ir": lambda k: row_z_relay(in_t, True, zs["i"]),
         "gz": grad_z, "iz": in_z, "dz": down_z, "dw": down_done,
         "H": make_hidden, "P": rs_a, "R": rs_b, "S": rs_c, "T": rs_d, "G": hg_b,
         "D": down_grad, "O": weight_grads,
@@ -495,10 +542,10 @@
             pltpu.VMEM((4, 256, W), F32),
             pltpu.VMEM((2, 256, W), BF),
             pltpu.VMEM((2, 2, 256, W), BF),
-            pltpu.VMEM((2, 256, NA), BF),
-            pltpu.VMEM((2, 256, NA), BF),
-            pltpu.VMEM((2, BW, D), BF),
-            pltpu.VMEM((NA, D), BF),
+            pltpu.VMEM((2, 256, NA - NS), BF),
+            pltpu.VMEM((2, 256, NA - NS), BF),
+            pltpu.VMEM((2, BW + NS // 2, D), BF),
+            pltpu.VMEM((NA - NS, D), BF),
             pltpu.VMEM((W, TOK), BF),
             pltpu.VMEM((TOK, 256), BF),
             pltpu.VMEM((TOK, 256), BF),

time: 184 us -> 174 us (0.946)
  Pallas kernels: 174 us -> 165 us
    pallas_call x1, Pallas kernels: 174 us -> 165 us  [on_device(): pl.pallas_call(kernel, name='swiglu_backward', out_shape=(jax.ShapeDtypeS...]
where the time goes in v3:
time: 174 us
  Pallas kernels  165 us (95%)
  local copies, waits for them, and re-layouts  9.06 us (5%)
    pallas_call x1, Pallas kernels, on_device(): pl.pallas_call(kernel, name='swiglu_backward', out_shape=(jax.ShapeDtypeS...  165 us
    unnamed x7, local copies, waits for them, and re-layouts  9.06 us

profile of v3, /device:TPU:0, one launch (start us, length us, event | category | flops | bytes accessed | tf_op | source)
XLA Modules:
  0.0 174.4 jit_solution(308118353021896856)
XLA Ops:
  0.6 164.6 %swiglu_backward.1 = (bf16[1024,1664]{1,0:T(8,128)(2,1)}, bf16[1024,1664]{1,0:T(8,128)(2,1)}, bf16[1664,1024]{1,0:T(8,128)(2,1)}) custom-call(bf16[128,1024]{1,0:T(8,128)(2,1)} %x_hbm.1, bf16[256,1664]{1,0:T(8,128)(2,1)} %gate_hbm.1, bf16[256,1664]{1,0:T(8,128)(2,1)} %up_hbm.1, bf16[128,1024]{1,0:T(8,128)(2,1)} %go_hbm.1, bf16[1664,1024]{1,0:T(8,128)(2,1)} %down_hbm.1), custom_call_target="tpu_custom_call" | custom-call | flops 27917287424 | bytes 41943040 | tf_op jit(solution)/shard_map/swiglu_backward/pallas_call | solution.py:525
  165.3 0.0 copy-start.1
  165.3 4.1 %copy.11 = bf16[1024,1664]{1,0:T(8,128)(2,1)} copy(bf16[1024,1664]{1,0:T(8,128)(2,1)} %get-tuple-element.6) | data formatting | bytes 6815744
  169.4 0.0 copy-done.1
  169.4 0.0 copy-start
  169.4 1.8 %copy.12 = bf16[1024,1664]{1,0:T(8,128)(2,1)} copy(bf16[1024,1664]{1,0:T(8,128)(2,1)S(1)} %copy-done.1) | data formatting | bytes 6815744
  171.2 1.4 copy-done
  172.6 1.7 %copy.13 = bf16[1664,1024]{1,0:T(8,128)(2,1)} copy(bf16[1664,1024]{1,0:T(8,128)(2,1)S(1)} %copy-done) | data formatting | bytes 6815744
Async XLA Ops:
  165.3 4.1 %copy-start.1 = (bf16[1024,1664]{1,0:T(8,128)(2,1)S(1)}, bf16[1024,1664]{1,0:T(8,128)(2,1)}, u32[]{:S(2)}) copy-start(bf16[1024,1664]{1,0:T(8,128)(2,1)} %get-tuple-element.7) | copy-start | bytes 10223620
  169.4 3.2 %copy-start = (bf16[1664,1024]{1,0:T(8,128)(2,1)S(1)}, bf16[1664,1024]{1,0:T(8,128)(2,1)}, u32[]{:S(2)}) copy-start(bf16[1664,1024]{1,0:T(8,128)(2,1)} %get-tuple-element.8) | copy-start | bytes 10223620

commit v4 on v3

--- a/solution.py
+++ b/solution.py
@@ -26,8 +26,11 @@
 OFFS = tuple(sum(CHUNKS[:i]) for i in range(len(CHUNKS)))
 NK = len(CHUNKS)
 assert NB + NA == FF
+FIRST_LATE = 3
+LATE = sum(CHUNKS[FIRST_LATE:])
+EARLY = FF - LATE
 N_REMOTE = 166
-N_LOCAL = 40
+N_LOCAL = 48
 
 
 SCHEDULE = (
@@ -57,7 +60,7 @@
 
 def kernel(
     x_hbm, gate_hbm, up_hbm, go_hbm, down_hbm,
-    og_hbm, ou_hbm, od_hbm,
+    og_hbm, ou_hbm, od_hbm, xt_hbm, late_g, late_u, late_h,
     grad, in_t, gate, up, gh, part, kept, far, near, swap_s, swap_r, dn_b, dn_a,
     hid_t, gg, gu, x_in, x_t, st_g, st_u, st_d,
     send_sem, recv_sem, local_sem,
@@ -280,9 +283,18 @@
         s = jax.nn.sigmoid(g)
         return g, u, s
 
+    keep = []
+
+    def keep_late(buf, hbm, k):
+        at = pl.ds(OFFS[k] - OFFS[FIRST_LATE], CHUNKS[k])
+        keep.append(local(buf.at[:, :, cols(k)], hbm.at[:, :, at]))
+
     def make_hidden(k):
         yc("g", k)
         yc("u", k)
+        if k >= FIRST_LATE:
+            keep_late(gate, late_g, k)
+            keep_late(up, late_u, k)
 
         def body(t, carry):
             g, u, s = silu_parts(t, k)
@@ -422,6 +434,9 @@
     def weight_grads(k):
         for copy in hb[k]:
             copy.wait_recv()
+        if k >= FIRST_LATE:
+            keep_late(gh, late_h, k)
+            return
         clear("g", k)
         clear("u", k)
         n = CHUNKS[k]
@@ -477,6 +492,11 @@
             waits = [zs["g"][1].wait_recv]
         rows[s + str(k)].first(waits)
 
+    def row_done(s, k):
+        rows[s + str(k)].done()
+        if s == "i":
+            keep.append(local(in_t.at[zl], xt_hbm))
+
     def down_z(k):
         zs["d"] = [send(down_hbm.at[src], dn_b.at[zl, dst], mate) for src, dst in down_parts(1 - zl)]
 
@@ -494,7 +514,7 @@
         "X": row_first,
         "F": lambda s, k: rows[s + str(k)].relay(),
         "L": lambda s, k: rows[s + str(k)].last(),
-        "E": lambda s, k: rows[s + str(k)].done(),
+        "E": row_done,
         "gr": lambda k: row_z_relay(grad, False, zs["g"]),
         "ir": lambda k: row_z_relay(in_t, True, zs["i"]),
         "gz": grad_z, "iz": in_z, "dz": down_z, "dw": down_done,
@@ -512,6 +532,8 @@
         for copy, is_remote in copies:
             if not is_remote:
                 copy.wait()
+    for copy in keep:
+        copy.wait()
     for copy in returned:
         copy.wait_recv()
     for copy in started:
@@ -520,18 +542,131 @@
     assert counts["remote"] <= N_REMOTE and counts["local"] <= N_LOCAL
 
 
+def late_kernel(
+    og_in, ou_in, od_in, xt_hbm, g_hbm, u_hbm, h_hbm,
+    og, ou, od,
+    xt, gate, up, gh, gg, gu, st_g, st_u, buf_g, buf_u, buf_d, sems,
+):
+    counts = [0]
+
+    def move(src, dst):
+        copy = pltpu.make_async_copy(src, dst, sems.at[counts[0]])
+        counts[0] += 1
+        return copy
+
+    def run(copies):
+        for copy in copies:
+            copy.start()
+
+    first = [move(h_hbm, gh), move(g_hbm, gate), move(u_hbm, up)]
+    second = [move(xt_hbm, xt)]
+    n = 2
+    loads, stores = {}, {}
+    early = pl.ds(0, EARLY)
+    for name, src, buf, dst in (
+        ("d", od_in, buf_d, od), ("g", og_in, buf_g, og), ("u", ou_in, buf_u, ou),
+    ):
+        part = src.shape[0] // n
+        loads[name], stores[name] = [], []
+        for j in range(n):
+            rows = pl.ds(j * part, part)
+            at = (rows, slice(None)) if name == "d" else (rows, early)
+            loads[name].append(move(src.at[at], buf.at[rows]))
+            stores[name].append(move(buf.at[rows], dst.at[at]))
+    run(first)
+    run(second)
+    for name in "dgu":
+        run(loads[name])
+    for copy in first:
+        copy.wait()
+
+    def elem(t, carry):
+        g = gate[t].astype(F32)
+        u = up[t].astype(F32)
+        e = gh[t].astype(F32)
+        s = jax.nn.sigmoid(g)
+        rows = pl.ds(pl.multiple_of(t * 256, 256), 256)
+        gu[rows] = (e * (g * s)).astype(BF)
+        gg[rows] = (e * u * s * (1.0 + g * (1.0 - s))).astype(BF)
+        return carry
+
+    def pass_on(name):
+        for load, store in zip(loads[name], stores[name]):
+            load.wait()
+            store.start()
+
+    def matmul(dst, rhs):
+        def body(m, carry):
+            w = pl.ds(pl.multiple_of(m * 512, 512), 512)
+            dst[w] = jnp.dot(xt[w, :], rhs[...], preferred_element_type=F32).astype(BF)
+            return carry
+
+        lax.fori_loop(0, D // 512, body, 0)
+
+    lax.fori_loop(0, 8, elem, 0)
+    for copy in second:
+        copy.wait()
+    pass_on("d")
+    matmul(st_g, gg)
+    out_g = move(st_g, og.at[:, pl.ds(EARLY, LATE)])
+    out_g.start()
+    pass_on("g")
+    pass_on("u")
+    matmul(st_u, gu)
+    out_u = move(st_u, ou.at[:, pl.ds(EARLY, LATE)])
+    out_u.start()
+    for name in "dgu":
+        for store in stores[name]:
+            store.wait()
+    out_g.wait()
+    out_u.wait()
+
+
+def finish(og, ou, od, xt, g, u, h):
+    any_spec = pl.BlockSpec(memory_space=pl.ANY)
+    return pl.pallas_call(
+        late_kernel,
+        name="late_grads",
+        out_shape=tuple(jax.ShapeDtypeStruct(a.shape, a.dtype) for a in (og, ou, od)),
+        in_specs=[any_spec] * 7,
+        out_specs=(any_spec,) * 3,
+        scratch_shapes=[
+            pltpu.VMEM((D, TOK), BF),
+            pltpu.VMEM((8, 256, LATE), BF),
+            pltpu.VMEM((8, 256, LATE), BF),
+            pltpu.VMEM((8, 256, LATE), BF),
+            pltpu.VMEM((TOK, LATE), BF),
+            pltpu.VMEM((TOK, LATE), BF),
+            pltpu.VMEM((D, LATE), BF),
+            pltpu.VMEM((D, LATE), BF),
+            pltpu.VMEM((D, EARLY), BF),
+            pltpu.VMEM((D, EARLY), BF),
+            pltpu.VMEM((FF, D), BF),
+            pltpu.SemaphoreType.DMA((24,)),
+        ],
+        compiler_params=pltpu.CompilerParams(vmem_limit_bytes=62 * 2**20),
+        cost_estimate=pl.CostEstimate(
+            flops=4 * TOK * D * LATE, bytes_accessed=28 * 2**20, transcendentals=TOK * LATE
+        ),
+    )(og, ou, od, xt, g, u, h)
+
+
 def on_device(inputs, gate_pre, up_pre, grad_out, down_weight):
     any_spec = pl.BlockSpec(memory_space=pl.ANY)
-    return pl.pallas_call(
+    return finish(*pl.pallas_call(
         kernel,
         name="swiglu_backward",
         out_shape=(
             jax.ShapeDtypeStruct((D, FF), BF),
             jax.ShapeDtypeStruct((D, FF), BF),
             jax.ShapeDtypeStruct((FF, D), BF),
+            jax.ShapeDtypeStruct((D, TOK), BF),
+            jax.ShapeDtypeStruct((8, 256, LATE), BF),
+            jax.ShapeDtypeStruct((8, 256, LATE), BF),
+            jax.ShapeDtypeStruct((8, 256, LATE), BF),
         ),
         in_specs=[any_spec] * 5,
-        out_specs=(any_spec,) * 3,
+        out_specs=(any_spec,) * 7,
         scratch_shapes=[
             pltpu.VMEM((2, TOK, D), BF),
             pltpu.VMEM((2, D, TOK), BF),
@@ -564,7 +699,7 @@
         cost_estimate=pl.CostEstimate(
             flops=8 * TOK * D * FF, bytes_accessed=40 * 2**20, transcendentals=TOK * FF
         ),
-    )(inputs, gate_pre, up_pre, grad_out, down_weight)
+    )(inputs, gate_pre, up_pre, grad_out, down_weight))
 
 
 def solution(mesh):

time: 174 us -> 173 us (level)
  local copies, waits for them, and re-layouts: 9.06 us -> 0 us
  Pallas kernels: 165 us -> 172 us
    pallas_call x0 -> x1, Pallas kernels: none -> 10.8 us  [finish(): pl.pallas_call(late_kernel, name='late_grads', out_shape=tuple((jax.Shape...]
    unnamed x7 -> x0, local copies, waits for them, and re-layouts: 9.06 us -> none
    pallas_call x1, Pallas kernels: 165 us -> 161 us  [on_device(): pl.pallas_call(kernel, name='swiglu_backward', out_shape=(jax.ShapeDtypeS...]
where the time goes in v4:
time: 173 us
  Pallas kernels  172 us (99%)
    pallas_call x1, Pallas kernels, on_device(): pl.pallas_call(kernel, name='swiglu_backward', out_shape=(jax.ShapeDtypeS...  161 us
    pallas_call x1, Pallas kernels, finish(): pl.pallas_call(late_kernel, name='late_grads', out_shape=tuple((jax.Shape...  10.8 us

profile of v4, /device:TPU:0, one launch (start us, length us, event | category | flops | bytes accessed | tf_op | source)
XLA Modules:
  0.0 172.7 jit_solution(9070947516543143016)
XLA Ops:
  0.6 161.0 %swiglu_backward.1 = (bf16[1024,1664]{1,0:T(8,128)(2,1)}, bf16[1024,1664]{1,0:T(8,128)(2,1)}, bf16[1664,1024]{1,0:T(8,128)(2,1)}, bf16[1024,2048]{1,0:T(8,128)(2...) custom-call(bf16[128,1024]{1,0:T(8,128)(2,1)} %x_hbm.1, ...), custom_call_target="tpu_custom_call" | custom-call | flops 27917287424 | bytes 41943040 | tf_op jit(solution)/shard_map/swiglu_backward/pallas_call | solution.py:656
  161.7 10.8 %late_grads.1 = (bf16[1024,1664]{1,0:T(8,128)(2,1)}, bf16[1024,1664]{1,0:T(8,128)(2,1)}, bf16[1664,1024]{1,0:T(8,128)(2,1)}) custom-call(bf16[1024,1664]{1,0:T(8,128)(2,1)} %get-tuple-element.10.og_in, bf16[1024,1664]{1,0:T(8,128)(2,1)} %get-tuple-element.11.ou_in, bf16[1664,1024]{1,0:T(8,128)(2,1)} %get-tuple-element.12.od_in, ...), custom_call_target="tpu_custom_call" | custom-call | flops 3221225472 | bytes 29360128 | tf_op jit(solution)/shard_map/late_grads/pallas_call | solution.py:627

commit v5 on v4

--- a/solution.py
+++ b/solution.py
@@ -34,15 +34,15 @@
 
 
 SCHEDULE = (
-    "Zu4", "Au0", "Zu1", "Ag0", "gz0", "Au4", "Au1", "Zg1", "gr0", "Zg0",
-    "Xg1", "Bu4", "Zu0", "Ag1", "Zg3", "Qg0", "iz0", "Zg2", "dz0", "Bu1",
-    "Ag3", "Qu0", "Bg1", "Xg0", "Fg0", "Bg0", "Bu0", "ir0", "Fg1", "Ag2",
-    "Lg0", "Eg0", "dw0", "P3", "H0", "H1", "Lg1", "Xi0", "P4", "R3",
-    "Zu2", "R4", "Eg1", "dw1", "P0", "S3", "P1", "Zg4", "Zu3", "D1",
-    "R0", "R1", "Fi0", "S0", "D0", "P2", "S4", "G0", "R2", "Li0",
-    "S1", "S2", "Au2", "Au3", "Ei0", "O0", "Bg3", "G1", "Bu3", "Bu2",
-    "Bg2", "T2", "O1", "Ag4", "H2", "D2", "G2", "H3", "T4", "Bg4",
-    "D3", "T3", "O2", "G4", "H4", "G3", "D4", "O4", "O3",
+    "Zg1", "gz0", "Ag0", "Au0", "Ag1", "Zg4", "Zu1", "gr0", "Zu2", "Xg1",
+    "Zu0", "Ag4", "Au1", "Zu3", "Bg4", "Zg0", "iz0", "dz0", "Qu0", "Xg0",
+    "Au2", "Au3", "Bu0", "Qg0", "Fg0", "Bu1", "ir0", "Fg1", "Bg1", "Bg0",
+    "Lg0", "Eg0", "dw0", "P4", "Lg1", "Xi0", "P3", "H1", "Zg2", "Eg1",
+    "dw1", "P2", "P0", "H0", "Zg3", "R3", "D1", "R0", "R2", "P1",
+    "S0", "Fi0", "Zu4", "S2", "S3", "D0", "R1", "R4", "G0", "Li0",
+    "S1", "Au4", "S4", "Ag3", "Ei0", "O0", "Ag2", "G1", "Bg3", "Bg2",
+    "Bu3", "T2", "Bu2", "Bu4", "O1", "T3", "H2", "T4", "H3", "G2",
+    "D2", "H4", "D3", "G3", "D4", "G4", "O2", "O3", "O4",
 )
 
 
@@ -307,31 +307,27 @@
     def nt(a, b):
         return lax.dot_general(a, b, (((1,), (1,)), ((), ())), preferred_element_type=F32)
 
-    def partial_block(k, t):
+    def partial_blocks(k, blocks):
         n = rs_width(k)
-        rows = pl.ds(al(t * 256, 256), 256)
+
+        def lhs(h):
+            return jnp.concatenate([grad[h, pl.ds(al(t * 256, 256), 256)] for t in blocks], axis=0)
+
         if is_b(k) or is_s(k):
-            acc = nt(grad[0, rows], dn_b[0, pl.ds(dn_at(k), n)])
-            return acc + nt(grad[1, rows], dn_b[1, pl.ds(dn_at(k), n)])
-        return nt(grad[zl, rows], dn_a[pl.ds(OFFS[k] - BW - NS, n)])
+            acc = nt(lhs(0), dn_b[0, pl.ds(dn_at(k), n)])
+            return acc + nt(lhs(1), dn_b[1, pl.ds(dn_at(k), n)])
+        return nt(lhs(zl), dn_a[pl.ds(OFFS[k] - BW - NS, n)])
 
     def make_sent(k):
-        def body(i, carry):
-            d = 2 - (i // 2) * (1 - 2 * (i % 2))
-            t = ((y + d) % 4) * 2 + (i // 2 + i) % 2
-            part[t, :, rcols(k)] = partial_block(k, t).astype(BF)
-            return carry
-
-        lax.fori_loop(0, 4, body, 0)
+        blocks = (y_far * 2, y_far * 2 + 1, y_next * 2 + 1, y_prev * 2)
+        acc = partial_blocks(k, blocks)
+        for i, t in enumerate(blocks):
+            part[t, :, rcols(k)] = acc[i * 256:(i + 1) * 256].astype(BF)
 
     def make_kept(k):
-        def body(i, carry):
-            d = (i // 2) * (1 + 2 * (i % 2))
-            t = ((y + d) % 4) * 2 + i % 2
-            kept[i, :, rcols(k)] = partial_block(k, t)
-            return carry
-
-        lax.fori_loop(0, 4, body, 0)
+        acc = partial_blocks(k, (y * 2, y * 2 + 1, y_next * 2, y_prev * 2 + 1))
+        for i in range(4):
+            kept[i, :, rcols(k)] = acc[i * 256:(i + 1) * 256]
 
     rs1, rs2, swaps, ha, hb = {}, {}, {}, {}, {}
 

time: 173 us -> 177 us (1.023)
  Pallas kernels: 172 us -> 176 us
    pallas_call x1, Pallas kernels: 161 us -> 165 us  [on_device(): pl.pallas_call(kernel, name='swiglu_backward', out_shape=(jax.ShapeDtypeS...]
where the time goes in v5:
time: 177 us
  Pallas kernels  176 us (99%)
    pallas_call x1, Pallas kernels, on_device(): pl.pallas_call(kernel, name='swiglu_backward', out_shape=(jax.ShapeDtypeS...  165 us
    pallas_call x1, Pallas kernels, finish(): pl.pallas_call(late_kernel, name='late_grads', out_shape=tuple((jax.Shape...  10.8 us

profile of v5, /device:TPU:0, one launch (start us, length us, event | category | flops | bytes accessed | tf_op | source)
XLA Modules:
  0.0 177.0 jit_solution(2238234012708506703)
XLA Ops:
  0.6 165.4 %swiglu_backward.1 = (bf16[1024,1664]{1,0:T(8,128)(2,1)}, bf16[1024,1664]{1,0:T(8,128)(2,1)}, bf16[1664,1024]{1,0:T(8,128)(2,1)}, bf16[1024,2048]{1,0:T(8,128)(2...) custom-call(bf16[128,1024]{1,0:T(8,128)(2,1)} %x_hbm.1, ...), custom_call_target="tpu_custom_call" | custom-call | flops 27917287424 | bytes 41943040 | tf_op jit(solution)/shard_map/swiglu_backward/pallas_call | solution.py:652
  166.0 10.8 %late_grads.1 = (bf16[1024,1664]{1,0:T(8,128)(2,1)}, bf16[1024,1664]{1,0:T(8,128)(2,1)}, bf16[1664,1024]{1,0:T(8,128)(2,1)}) custom-call(bf16[1024,1664]{1,0:T(8,128)(2,1)} %get-tuple-element.10.og_in, bf16[1024,1664]{1,0:T(8,128)(2,1)} %get-tuple-element.11.ou_in, bf16[1664,1024]{1,0:T(8,128)(2,1)} %get-tuple-element.12.od_in, ...), custom_call_target="tpu_custom_call" | custom-call | flops 3221225472 | bytes 29360128 | tf_op jit(solution)/shard_map/late_grads/pallas_call | solution.py:623

commit v6 on v4

--- a/solution.py
+++ b/solution.py
@@ -558,7 +558,11 @@
         for copy in copies:
             copy.start()
 
-    first = [move(h_hbm, gh), move(g_hbm, gate), move(u_hbm, up)]
+    first = [
+        [move(src.at[pl.ds(i * 4, 4)], dst.at[pl.ds(i * 4, 4)]) for src, dst in
+         ((h_hbm, gh), (g_hbm, gate), (u_hbm, up))]
+        for i in range(2)
+    ]
     second = [move(xt_hbm, xt)]
     n = 2
     loads, stores = {}, {}
@@ -573,12 +577,11 @@
             at = (rows, slice(None)) if name == "d" else (rows, early)
             loads[name].append(move(src.at[at], buf.at[rows]))
             stores[name].append(move(buf.at[rows], dst.at[at]))
-    run(first)
+    run(first[0])
+    run(first[1])
     run(second)
     for name in "dgu":
         run(loads[name])
-    for copy in first:
-        copy.wait()
 
     def elem(t, carry):
         g = gate[t].astype(F32)
@@ -596,14 +599,12 @@
             store.start()
 
     def matmul(dst, rhs):
-        def body(m, carry):
-            w = pl.ds(pl.multiple_of(m * 512, 512), 512)
-            dst[w] = jnp.dot(xt[w, :], rhs[...], preferred_element_type=F32).astype(BF)
-            return carry
-
-        lax.fori_loop(0, D // 512, body, 0)
-
-    lax.fori_loop(0, 8, elem, 0)
+        dst[...] = jnp.dot(xt[...], rhs[...], preferred_element_type=F32).astype(BF)
+
+    for i in range(2):
+        for copy in first[i]:
+            copy.wait()
+        lax.fori_loop(i * 4, i * 4 + 4, elem, 0)
     for copy in second:
         copy.wait()
     pass_on("d")

time: 173 us -> 173 us (level)
  no operation moved by 1% of the time
where the time goes in v6:
time: 173 us; the launch traced here: 172 us
  Pallas kernels  172 us (99%)
    pallas_call x1, Pallas kernels, on_device(): pl.pallas_call(kernel, name='swiglu_backward', out_shape=(jax.ShapeDtypeS...  161 us
    pallas_call x1, Pallas kernels, finish(): pl.pallas_call(late_kernel, name='late_grads', out_shape=tuple((jax.Shape...  10.7 us

profile of v6, /device:TPU:0, one launch (start us, length us, event | category | flops | bytes accessed | tf_op | source)
XLA Modules:
  0.0 172.5 jit_solution(6388045857086616866)
XLA Ops:
  0.6 161.0 %swiglu_backward.1 = (bf16[1024,1664]{1,0:T(8,128)(2,1)}, bf16[1024,1664]{1,0:T(8,128)(2,1)}, bf16[1664,1024]{1,0:T(8,128)(2,1)}, bf16[1024,2048]{1,0:T(8,128)(2...) custom-call(bf16[128,1024]{1,0:T(8,128)(2,1)} %x_hbm.1, ...), custom_call_target="tpu_custom_call" | custom-call | flops 27917287424 | bytes 41943040 | tf_op jit(solution)/shard_map/swiglu_backward/pallas_call | solution.py:657
  161.7 10.7 %late_grads.1 = (bf16[1024,1664]{1,0:T(8,128)(2,1)}, bf16[1024,1664]{1,0:T(8,128)(2,1)}, bf16[1664,1024]{1,0:T(8,128)(2,1)}) custom-call(bf16[1024,1664]{1,0:T(8,128)(2,1)} %get-tuple-element.10.og_in, bf16[1024,1664]{1,0:T(8,128)(2,1)} %get-tuple-element.11.ou_in, bf16[1664,1024]{1,0:T(8,128)(2,1)} %get-tuple-element.12.od_in, ...), custom_call_target="tpu_custom_call" | custom-call | flops 3221225472 | bytes 29360128 | tf_op jit(solution)/shard_map/late_grads/pallas_call | solution.py:628
